TPU v7x, 512 devices: a whole 4x4x16 slice. The times are simulated.
512 devices in a mesh: dp: 16 (over z), pts: 32 (over x, y, core).
Axes of the slice: x: 4, y: 4, z: 16, core: 2. Of those that a mesh axis runs over, the one named last changes fastest.
Arguments:
- x_mid: bfloat16 [98304, 1024], P(('dp', 'pts')), parts along dimension 0, may hold values from -30 to 30
- fx_mid: bfloat16 [98304, 1024], P(('dp', 'pts')), parts along dimension 0, may hold values from -20 to 20
- gumbel: bfloat16 [98304, 8192], P(('dp', 'pts')), parts along dimension 0, may hold values from -2.5 to 240
- w_slice: bfloat16 [64, 512], replicated, may hold values from -0.75 to 0.75
- w_temp: bfloat16 [64], replicated, may hold values from -0.75 to 0.75
- query_weight: float32 [64, 64], replicated, may hold values from -12 to 12
- key_weight: float32 [64, 64], replicated, may hold values from -12 to 12
- value_weight: float32 [64, 64], replicated, may hold values from -1.5 to 1.5
Outputs:
- sliced_out: bfloat16 [98304, 1024], P(('dp', 'pts')), parts along dimension 0
There are 16 independent parts, one for each index of `dp`. A program takes and returns all parts, laid end to end along the dimension named above; an argument that names none is the same for every part. Nothing has to cross between parts.
All inputs are finite; a program needn't handle non-finite values.
Results may differ from a plain program's by a relative error of at most 0.0065.
The roundings to bfloat16 on the way count: a program that leaves them out, or rounds other values in their place, can miss the bound.
Values may be sent and summed in bfloat16 or wider, within the bound.
No kernel may reach another device: no remote copies, remote signals or barrier semaphores. Data moves between devices by JAX's collectives and lax.ppermute only.
A program may use at most 64 MiB of HBM per device.

v0:
```python
import math

import jax
import jax.numpy as jnp
from jax import lax
from jax.sharding import PartitionSpec as P

H = 16
DH = 64
M = 512


epsilon = 1e-05
highest_precision = lax.Precision.HIGHEST


def slice_weights(x_mid, gumbel, w_slice, w_temp):
    count_rows = x_mid.shape[0]
    heads_view = x_mid.reshape(count_rows, H, DH)
    logits = jnp.einsum("phd,dm->phm", heads_view, w_slice, preferred_element_type=jnp.float32)
    temper = 0.5 + jax.nn.softplus(
        jnp.einsum("phd,d->ph", heads_view, w_temp, preferred_element_type=jnp.float32)
    )
    logits = (logits + gumbel.reshape(count_rows, H, M).astype(jnp.float32)) / temper[:, :, None]
    return jax.nn.softmax(logits, axis=-1)


def project(slice_token_state, matrix):
    return jnp.einsum("rjd,de->rje", slice_token_state, matrix, precision=highest_precision)


def attend_pair(element):
    query_matrix, keys_pair, values_pair = element
    scores = jnp.einsum("qjd,kjd->jqk", query_matrix, keys_pair, precision=highest_precision) * (
        1.0 / math.sqrt(DH)
    )
    attn_probs = jax.nn.softmax(scores, axis=-1)
    return jnp.einsum("jqk,kjd->qjd", attn_probs, values_pair, precision=highest_precision)


def on_device(x_mid, fx_mid, gumbel, w_slice, w_temp, query_weight, key_weight, value_weight):
    count_rows = x_mid.shape[0]
    pair_count = H // 2
    weights = slice_weights(x_mid, gumbel, w_slice, w_temp)
    slice_assignment = weights.astype(jnp.bfloat16).reshape(count_rows, pair_count, 2, M)
    masses = jnp.sum(weights, axis=0).reshape(pair_count, 2, M)
    masses = jnp.transpose(masses, (0, 2, 1)).reshape(pair_count * M, 2)
    value_matrix = fx_mid.reshape(count_rows, pair_count, 2, DH)
    pooled_features = jnp.einsum(
        "npjm,npjd->pmjd", slice_assignment, value_matrix, preferred_element_type=jnp.float32
    )
    pooled_features = pooled_features.reshape(pair_count * M, 2 * DH)
    pooled_features, masses = lax.psum((pooled_features, masses), "pts")
    slice_token_state = (pooled_features / (jnp.repeat(masses, DH, axis=1) + epsilon)).reshape(
        pair_count * M, 2, DH
    )
    query_matrix = project(slice_token_state, query_weight).reshape(pair_count, M, 2, DH)
    gathered_keys = project(slice_token_state, key_weight).reshape(pair_count, M, 2, DH)
    gathered_values = project(slice_token_state, value_weight).reshape(pair_count, M, 2, DH)
    attention_output = lax.map(attend_pair, (query_matrix, gathered_keys, gathered_values)).astype(
        jnp.bfloat16
    )
    sliced = jnp.einsum(
        "npjm,pmjd->npjd", slice_assignment, attention_output, preferred_element_type=jnp.float32
    )
    return sliced.reshape(count_rows, H * DH).astype(jnp.bfloat16)


def solution(mesh):
    return jax.shard_map(
        on_device,
        mesh=mesh,
        in_specs=(
            P(("dp", "pts"), None),
            P(("dp", "pts"), None),
            P(("dp", "pts"), None),
            P(),
            P(),
            P(),
            P(),
            P(),
        ),
        out_specs=P(("dp", "pts"), None),
        check_vma=False,
    )
```

profile of v0, /device:TPU:1, one launch (start us, length us, event | category | flops | bytes accessed | tf_op | source)
XLA Modules:
  0.0 302.2 jit_solution(6494436658826723043)
XLA Ops:
  8.4 5.9 %copy.29 = f32[24,8,16,512]{3,2,1,0:T(8,128)} copy(bf16[24,8,16,512]{3,1,2,0:T(8,128)(2,1)} %bitcast.107) | data formatting | bytes 9437184
  14.7 3.7 %bitcast_add_fusion = f32[192,16,512]{2,1,0:T(8,128)S(1)} fusion(f32[24,8,16,512]{3,2,1,0:T(8,128)} %copy.29, bf16[192,16,64]{2,1,0:T(8,128)(2,1)S(1)} %copy.16, bf16[64,512]{1,0:T(8,128)(2,1)S(1)} %copy-done), kind=kOutput, calls=%fused_computation.21 | convolution fusion | flops 202899456 | bytes 13041664 | tf_op jit(solution)/shard_map/phd,dm->phm/dot_general | solution.py:20
  18.5 47.4 %fusion.44 = (f32[192,16]{1,0:T(8,128)S(1)}, f32[192,16,512]{2,1,0:T(8,128)S(1)}) fusion(f32[192,16,512]{2,1,0:T(8,128)S(1)} %bitcast_add_fusion, f32[192,16]{1,0:T(8,128)S(1)} %fusion.33), kind=kOutput, calls=%fused_computation.53 | output fusion | flops 4719103 | bytes 12607488 | tf_op jit(solution)/shard_map/sub | solution.py:25
  66.7 1.8 copy.28
  68.5 2.0 copy.17
  70.5 1.7 convolution_bitcast_fusion
  73.5 2.9 copy.30
  76.5 125.3 %psum.15 = f32[4096,2]{0,1:T(2,128)S(1)} all-reduce(f32[4096,2]{0,1:T(2,128)S(1)} %bitcast.110), channel_id=1, replica_groups=mesh['dp'=16,'pts'=32] {'pts'}, use_global_device_ids=true, to_apply=%region_4.5 | all-reduce | flops 8192 | bytes 65536 | tf_op jit(solution)/shard_map/psum | solution.py:53
  201.8 18.3 %all-reduce.2.cloned.1.call-done = f32[4096,128]{0,1:T(8,128)} async-done(((f32[4096,128]{0,1:T(8,128)}), f32[4096,128]{0,1:T(8,128)}) %all-reduce.2.cloned.1.call-update) | async-done | bytes 2097168 | tf_op jit(solution)/shard_map/psum | solution.py:53
  220.1 1.8 bitcast_divide_fusion
  223.6 4.7 %fusion.26 = f32[8,512,2,64]{1,3,2,0:T(8,128)} fusion(f32[8,512,2,64]{1,0,3,2:T(8,128)S(1)} %bitcast.97, f32[64,64]{1,0:T(8,128)S(1)} %copy-done.1), kind=kOutput, calls=%fused_computation.29 | convolution fusion | flops 402653184 | bytes 4210688 | tf_op jit(solution)/shard_map/rjd,de->rje/dot_general | solution.py:29
  228.3 4.6 %fusion.28 = f32[8,512,2,64]{1,3,2,0:T(8,128)} fusion(f32[8,512,2,64]{1,0,3,2:T(8,128)S(1)} %bitcast.98, f32[64,64]{1,0:T(8,128)S(1)} %copy-done.2), kind=kOutput, calls=%fused_computation.31 | convolution fusion | flops 402653184 | bytes 4210688 | tf_op jit(solution)/shard_map/rjd,de->rje/dot_general | solution.py:29
  232.9 4.7 %fusion.30 = f32[8,512,2,64]{1,3,2,0:T(8,128)} fusion(f32[8,512,2,64]{1,0,3,2:T(8,128)S(1)} %bitcast.99, f32[64,64]{1,0:T(8,128)S(1)} %copy-done.3), kind=kOutput, calls=%fused_computation.33 | convolution fusion | flops 402653184 | bytes 4210688 | tf_op jit(solution)/shard_map/rjd,de->rje/dot_general | solution.py:29
  237.6 52.7 %while.10 = (s32[]{:T(128)}, bf16[8,512,2,64]{1,3,2,0:T(8,128)(2,1)}, f32[8,512,2,64]{1,3,2,0:T(8,128)}, f32[8,512,2,64]{1,3,2,0:T(8,128)}, f32[8,512,2,64]{1,3,2,0:T(8,128)}, /*index=5*/s32[]{:T(128)}) while((s32[]{:T(128)}, bf16[8,512,2,64]{1,3,2,0:T(8,128)(2,1)}, f32[8,512,2,64]{1,3,2,0:T(8,128)}, f32[8,512,2,64]{1,3,2,0:T(8,128)}, ...), condition=%wide.region_8.9_spmd, body=%wide.region_5.8_spmd.sunk | while | flops 809498624 | bytes 7362629 | solution.py:60
  237.6 2.9 multiply_reduce_fusion.2
  240.9 3.3 %fusion.58 = bf16[8,512,2,64]{1,3,2,0:T(8,128)(2,1)} fusion(bf16[8,512,2,64]{1,3,2,0:T(8,128)(2,1)} %get-tuple-element.91, s32[]{:T(128)} %get-tuple-element.90, f32[2,512,512]{1,2,0:T(8,128)S(1)} %get-tuple-element.82, f32[2,512]{1,0:T(2,128)S(1)} %fusion.57, f32[2,512]{1,0:T(2,128)S(1)} %get-tuple-element.83, f32[8,512,2,64]{1,3,2,0:T(8,128)} %get-tuple-element.98), kind=kOutput, calls=%fused_computation.6.clone.1 | convolution fusion | flops 404226048 | bytes 2630656 | tf_op jit(solution)/shard_map/while/body/eval_jaxpr/jqk,kjd->qjd/dot_general | solution.py:38
  244.2 2.9 multiply_reduce_fusion.2
  247.5 3.3 %fusion.58 = bf16[8,512,2,64]{1,3,2,0:T(8,128)(2,1)} fusion(bf16[8,512,2,64]{1,3,2,0:T(8,128)(2,1)} %get-tuple-element.91, s32[]{:T(128)} %get-tuple-element.90, f32[2,512,512]{1,2,0:T(8,128)S(1)} %get-tuple-element.82, f32[2,512]{1,0:T(2,128)S(1)} %fusion.57, f32[2,512]{1,0:T(2,128)S(1)} %get-tuple-element.83, f32[8,512,2,64]{1,3,2,0:T(8,128)} %get-tuple-element.98), kind=kOutput, calls=%fused_computation.6.clone.1 | convolution fusion | flops 404226048 | bytes 2630656 | tf_op jit(solution)/shard_map/while/body/eval_jaxpr/jqk,kjd->qjd/dot_general | solution.py:38
  250.8 2.9 multiply_reduce_fusion.2
  254.0 3.3 %fusion.58 = bf16[8,512,2,64]{1,3,2,0:T(8,128)(2,1)} fusion(bf16[8,512,2,64]{1,3,2,0:T(8,128)(2,1)} %get-tuple-element.91, s32[]{:T(128)} %get-tuple-element.90, f32[2,512,512]{1,2,0:T(8,128)S(1)} %get-tuple-element.82, f32[2,512]{1,0:T(2,128)S(1)} %fusion.57, f32[2,512]{1,0:T(2,128)S(1)} %get-tuple-element.83, f32[8,512,2,64]{1,3,2,0:T(8,128)} %get-tuple-element.98), kind=kOutput, calls=%fused_computation.6.clone.1 | convolution fusion | flops 404226048 | bytes 2630656 | tf_op jit(solution)/shard_map/while/body/eval_jaxpr/jqk,kjd->qjd/dot_general | solution.py:38
  257.3 2.9 multiply_reduce_fusion.2
  260.6 3.3 %fusion.58 = bf16[8,512,2,64]{1,3,2,0:T(8,128)(2,1)} fusion(bf16[8,512,2,64]{1,3,2,0:T(8,128)(2,1)} %get-tuple-element.91, s32[]{:T(128)} %get-tuple-element.90, f32[2,512,512]{1,2,0:T(8,128)S(1)} %get-tuple-element.82, f32[2,512]{1,0:T(2,128)S(1)} %fusion.57, f32[2,512]{1,0:T(2,128)S(1)} %get-tuple-element.83, f32[8,512,2,64]{1,3,2,0:T(8,128)} %get-tuple-element.98), kind=kOutput, calls=%fused_computation.6.clone.1 | convolution fusion | flops 404226048 | bytes 2630656 | tf_op jit(solution)/shard_map/while/body/eval_jaxpr/jqk,kjd->qjd/dot_general | solution.py:38
  263.9 2.9 multiply_reduce_fusion.2
  267.2 3.3 %fusion.58 = bf16[8,512,2,64]{1,3,2,0:T(8,128)(2,1)} fusion(bf16[8,512,2,64]{1,3,2,0:T(8,128)(2,1)} %get-tuple-element.91, s32[]{:T(128)} %get-tuple-element.90, f32[2,512,512]{1,2,0:T(8,128)S(1)} %get-tuple-element.82, f32[2,512]{1,0:T(2,128)S(1)} %fusion.57, f32[2,512]{1,0:T(2,128)S(1)} %get-tuple-element.83, f32[8,512,2,64]{1,3,2,0:T(8,128)} %get-tuple-element.98), kind=kOutput, calls=%fused_computation.6.clone.1 | convolution fusion | flops 404226048 | bytes 2630656 | tf_op jit(solution)/shard_map/while/body/eval_jaxpr/jqk,kjd->qjd/dot_general | solution.py:38
  270.5 2.9 multiply_reduce_fusion.2
  273.8 3.3 %fusion.58 = bf16[8,512,2,64]{1,3,2,0:T(8,128)(2,1)} fusion(bf16[8,512,2,64]{1,3,2,0:T(8,128)(2,1)} %get-tuple-element.91, s32[]{:T(128)} %get-tuple-element.90, f32[2,512,512]{1,2,0:T(8,128)S(1)} %get-tuple-element.82, f32[2,512]{1,0:T(2,128)S(1)} %fusion.57, f32[2,512]{1,0:T(2,128)S(1)} %get-tuple-element.83, f32[8,512,2,64]{1,3,2,0:T(8,128)} %get-tuple-element.98), kind=kOutput, calls=%fused_computation.6.clone.1 | convolution fusion | flops 404226048 | bytes 2630656 | tf_op jit(solution)/shard_map/while/body/eval_jaxpr/jqk,kjd->qjd/dot_general | solution.py:38
  277.1 2.9 multiply_reduce_fusion.2
  280.4 3.3 %fusion.58 = bf16[8,512,2,64]{1,3,2,0:T(8,128)(2,1)} fusion(bf16[8,512,2,64]{1,3,2,0:T(8,128)(2,1)} %get-tuple-element.91, s32[]{:T(128)} %get-tuple-element.90, f32[2,512,512]{1,2,0:T(8,128)S(1)} %get-tuple-element.82, f32[2,512]{1,0:T(2,128)S(1)} %fusion.57, f32[2,512]{1,0:T(2,128)S(1)} %get-tuple-element.83, f32[8,512,2,64]{1,3,2,0:T(8,128)} %get-tuple-element.98), kind=kOutput, calls=%fused_computation.6.clone.1 | convolution fusion | flops 404226048 | bytes 2630656 | tf_op jit(solution)/shard_map/while/body/eval_jaxpr/jqk,kjd->qjd/dot_general | solution.py:38
  283.7 2.9 multiply_reduce_fusion.2
  287.0 3.3 %fusion.58 = bf16[8,512,2,64]{1,3,2,0:T(8,128)(2,1)} fusion(bf16[8,512,2,64]{1,3,2,0:T(8,128)(2,1)} %get-tuple-element.91, s32[]{:T(128)} %get-tuple-element.90, f32[2,512,512]{1,2,0:T(8,128)S(1)} %get-tuple-element.82, f32[2,512]{1,0:T(2,128)S(1)} %fusion.57, f32[2,512]{1,0:T(2,128)S(1)} %get-tuple-element.83, f32[8,512,2,64]{1,3,2,0:T(8,128)} %get-tuple-element.98), kind=kOutput, calls=%fused_computation.6.clone.1 | convolution fusion | flops 404226048 | bytes 2630656 | tf_op jit(solution)/shard_map/while/body/eval_jaxpr/jqk,kjd->qjd/dot_general | solution.py:38
  290.3 3.1 %convolution_convert_fusion = bf16[8,2,64,192]{3,2,1,0:T(8,128)(2,1)} fusion(bf16[192,8,2,512]{3,0,2,1:T(8,128)(2,1)S(1)} %bitcast.101, bf16[8,512,2,64]{1,3,2,0:T(8,128)(2,1)} %get-tuple-element.32), kind=kOutput, calls=%fused_computation.36 | convolution fusion | flops 201523200 | bytes 4587520 | tf_op jit(solution)/shard_map/npjm,pmjd->npjd/dot_general | solution.py:63
  293.4 2.0 copy.21
  (31 shorter events, 8.9 us)
Async XLA Ops:
  6.5 8.2 %copy-start = (bf16[64,512]{1,0:T(8,128)(2,1)S(1)}, bf16[64,512]{1,0:T(8,128)(2,1)}, u32[]{:S(2)}) copy-start(bf16[64,512]{1,0:T(8,128)(2,1)} %param.13) | copy-start | bytes 196612
  6.5 213.6 %all-reduce.2.cloned.1.call-start = ((), (), s32[]{:S(2)}) async-start(), calls=%async_computation | async-start | bytes 4194304 | tf_op jit(solution)/shard_map/psum | solution.py:53
  8.4 5.9 %copy-start.4 = (bf16[64]{0:T(256)(128)(2,1)S(1)}, bf16[64]{0:T(256)(128)(2,1)}, u32[]{:S(2)}) copy-start(bf16[64]{0:T(256)(128)(2,1)} %param.14) | copy-start | bytes 388
  221.9 1.7 copy-start.1
  223.6 4.7 %copy-start.2 = (f32[64,64]{1,0:T(8,128)S(1)}, f32[64,64]{1,0:T(8,128)}, u32[]{:S(2)}) copy-start(f32[64,64]{1,0:T(8,128)} %param.15) | copy-start | bytes 49156
  228.3 4.6 %copy-start.3 = (f32[64,64]{1,0:T(8,128)S(1)}, f32[64,64]{1,0:T(8,128)}, u32[]{:S(2)}) copy-start(f32[64,64]{1,0:T(8,128)} %param.17) | copy-start | bytes 49156
Sparse Core Ops, SparseCore 0:
  76.5 143.5 all-reduce.1
where the time goes:
time: 303 us; the launch traced here: 302 us
  blocking collectives  125 us (41%)
  matrix products  72.5 us (24%)
  other arithmetic  53 us (17%)
  local copies, waits for them, and re-layouts  19.5 us (6%)
  waiting for transfers between devices  18.3 us (6%)
  between operations  13.5 us (4%)
    psum x1, blocking collectives, on_device(): pooled_features, masses = lax.psum((pooled_features, masses), 'pts')  125 us
    sub x1, other arithmetic, slice_weights(): return jax.nn.softmax(logits, axis=-1)  47.4 us
    dot_general x8, matrix products, attend_pair(): jnp.einsum('jqk,kjd->qjd', attn_probs, values_pair, precision=highest_pre...  26.4 us
    dot_general x8, matrix products, attend_pair(): jnp.einsum('qjd,kjd->jqk', query_matrix, keys_pair, precision=highest_pre...  23.3 us
    psum x1, waiting for transfers between devices, on_device(): pooled_features, masses = lax.psum((pooled_features, masses), 'pts')  18.3 us
    dot_general x3, matrix products, project(): jnp.einsum('rjd,de->rje', slice_token_state, matrix, precision=highest_pr...  14 us
    unnamed x15, local copies, waits for them, and re-layouts  13.8 us
  transfers between devices with their start and end apart: 1, of which 1 were waited for; matrix products, arithmetic and copies ran while one was open for 0% of the time, Pallas kernels for 0%

commit v1 on v0

v1 whole, which is shorter than its diff:
```python
import math

import jax
import jax.numpy as jnp
from jax import lax
from jax.experimental import pallas as pl
from jax.experimental.pallas import tpu as pltpu
from jax.sharding import Mesh, PartitionSpec as P

H = 16
DH = 64
M = 512
HALF = M // 2
LANES = 128
TILES = M // LANES
GROUP = 8
GROUPS = H // GROUP
BATCH = 4
BATCHES = H // BATCH
FEATURES = TILES * DH
SUMS = FEATURES + 2 * TILES
ROWS = FEATURES + 16
SPAN = 120.0
STEP = 64
EPS = 1e-05
LOG2E = 1.0 / math.log(2.0)
f32 = jnp.float32
bf16 = jnp.bfloat16
IN_HBM = pl.BlockSpec(memory_space=pltpu.HBM)
IN_VMEM = pl.BlockSpec(memory_space=pltpu.VMEM)


def dot(a, b):
    return jnp.dot(a, b, preferred_element_type=f32)


def dot_nt(a, b):
    return lax.dot_general(a, b, (((1,), (1,)), ((), ())), preferred_element_type=f32)


def dot_tn(a, b):
    return lax.dot_general(a, b, (((0,), (0,)), ((), ())), preferred_element_type=f32)


def last_rows(mass, peak):
    high = mass.astype(bf16).astype(f32)
    row = lax.broadcasted_iota(jnp.int32, (16, LANES), 0)
    rows = jnp.zeros((16, LANES), f32)
    for k, part in enumerate((high, mass - high, peak)):
        for t in range(TILES):
            rows = jnp.where(row == k * TILES + t, part[:, t * LANES : (t + 1) * LANES], rows)
    return rows.astype(bf16)


def pool_kernel(
    x_hbm, fx_hbm, g_hbm, ws_hbm, wt_hbm, shares_hbm, sums_hbm,
    x_ref, fx_ref, g_ref, ws_ref, wt_ref, scale_ref, features_ref, logit_ref, shares_ref, sums_ref,
    sems, g_sems, out_sems,
):
    points = x_hbm.shape[0]

    def fetch(group):
        columns = pl.ds(group * (GROUP * M), GROUP * M)
        return pltpu.make_async_copy(g_hbm.at[:, columns], g_ref.at[group], g_sems.at[group])

    def results(batch):
        heads = pl.ds(batch * BATCH, BATCH)
        return (
            pltpu.make_async_copy(shares_ref.at[heads], shares_hbm.at[heads], out_sems.at[0, batch]),
            pltpu.make_async_copy(sums_ref.at[heads], sums_hbm.at[heads], out_sems.at[1, batch]),
        )

    first = [
        pltpu.make_async_copy(hbm, ref, sems.at[k])
        for k, (hbm, ref) in enumerate(((wt_hbm, wt_ref), (ws_hbm, ws_ref), (x_hbm, x_ref), (fx_hbm, fx_ref)))
    ]
    for copy in first:
        copy.start()
    for group in range(GROUPS):
        fetch(group).start()
    first[0].wait()
    wt = jnp.transpose(jnp.broadcast_to(wt_ref[...].astype(f32), (LANES, DH)))
    lane = lax.broadcasted_iota(jnp.int32, (DH, LANES), 1)
    wt = jnp.concatenate([jnp.where(lane == j, wt, 0.0) for j in range(H)], axis=0).astype(bf16)
    first[1].wait()
    ws = ws_ref[...]
    zero = jnp.zeros_like(ws)
    ws = (jnp.concatenate([ws, zero], axis=0), jnp.concatenate([zero, ws], axis=0))
    first[2].wait()
    v = dot(x_ref[...], wt)
    temper = 0.5 + jnp.maximum(v, 0.0) + jnp.log1p(jnp.exp(-jnp.abs(v)))
    scale = LOG2E / temper
    for group in range(GROUPS):
        scale_ref[group] = scale if group == 0 else pltpu.roll(scale, LANES - group * GROUP, 1)
    pairs = jnp.concatenate([x_ref[:, pl.ds(p * LANES, LANES)] for p in range(H // 2)], axis=0)
    for parity in range(2):
        logits = dot(pairs, ws[parity])
        for p in range(H // 2):
            logit_ref[2 * p + parity] = logits[p * points : (p + 1) * points]
    first[3].wait()
    features = jnp.transpose(fx_ref[...].astype(f32)).astype(bf16)
    for head in range(H):
        features_ref[head] = features[head * DH : (head + 1) * DH]

    def one_group(group, carry):
        fetch(group).wait()
        scale = scale_ref[group]
        for j0 in range(0, GROUP, BATCH):
            heads = range(j0, j0 + BATCH)
            totals = []
            for j in heads:
                head = group * GROUP + j
                for r in range(0, points, STEP):
                    rows = pl.ds(r, STEP)
                    logits = logit_ref[head, rows, :] + g_ref[group, rows, pl.ds(j * M, M)].astype(f32)
                    top = jnp.max(logits, axis=1, keepdims=True)
                    e = jnp.exp2((logits - top) * scale[r : r + STEP, j : j + 1])
                    logit_ref[head, rows, :] = e
                    total = (e[:, :LANES] + e[:, LANES : 2 * LANES]) + (e[:, 2 * LANES : 3 * LANES] + e[:, 3 * LANES :])
                    high = total.astype(bf16)
                    low = (total - high.astype(f32)).astype(bf16)
                    totals.append(jnp.concatenate([high, low], axis=1))
            totals = 1.0 / dot(jnp.concatenate(totals, axis=0), jnp.ones((2 * LANES, LANES), bf16))
            masses = []
            for b, j in enumerate(heads):
                head = group * GROUP + j
                mass = jnp.zeros((8, M), f32)
                total = totals[b * points : (b + 1) * points]
                for r in range(0, points, STEP):
                    rows = pl.ds(r, STEP)
                    share = logit_ref[head, rows, :] * jnp.concatenate([total[r : r + STEP]] * TILES, axis=1)
                    for k in range(0, STEP, 8):
                        mass = mass + share[k : k + 8]
                    shares_ref[head, rows, :] = share.astype(bf16)
                masses.append(jnp.sum(mass, axis=0, keepdims=True))
            for b, j in enumerate(heads):
                head = group * GROUP + j
                pooled = dot(features_ref[head], shares_ref[head])
                peak = jnp.maximum(jnp.max(jnp.abs(pooled), axis=0, keepdims=True), 1e-30)
                peak = peak.astype(bf16).astype(f32)
                pooled = jnp.exp2(pooled * (SPAN / peak))
                for t in range(TILES):
                    tile = pooled[:, t * LANES : (t + 1) * LANES]
                    sums_ref[head, pl.ds(t * DH, DH), :] = tile.astype(bf16)
                sums_ref[head, pl.ds(FEATURES, 16), :] = last_rows(masses[b], peak)
            for copy in results(group * (GROUP // BATCH) + j0 // BATCH):
                copy.start()
        return carry

    lax.fori_loop(0, GROUPS, one_group, 0)
    for batch in range(BATCHES):
        for copy in results(batch):
            copy.wait()


def pool(x_mid, fx_mid, gumbel, w_slice, w_temp):
    points = x_mid.shape[0]
    return pl.pallas_call(
        pool_kernel,
        out_shape=(
            jax.ShapeDtypeStruct((H, points, M), bf16),
            jax.ShapeDtypeStruct((H, ROWS, LANES), bf16),
        ),
        in_specs=[IN_HBM] * 5,
        out_specs=(IN_HBM, IN_HBM),
        scratch_shapes=[
            pltpu.VMEM((points, H * DH), bf16),
            pltpu.VMEM((points, H * DH), bf16),
            pltpu.VMEM((GROUPS, points, GROUP * M), bf16),
            pltpu.VMEM((DH, M), bf16),
            pltpu.VMEM((1, DH), bf16),
            pltpu.VMEM((GROUPS, points, LANES), f32),
            pltpu.VMEM((H, DH, points), bf16),
            pltpu.VMEM((H, points, M), f32),
            pltpu.VMEM((H, points, M), bf16),
            pltpu.VMEM((H, ROWS, LANES), bf16),
            pltpu.SemaphoreType.DMA((4,)),
            pltpu.SemaphoreType.DMA((GROUPS,)),
            pltpu.SemaphoreType.DMA((2, BATCHES)),
        ],
        compiler_params=pltpu.CompilerParams(vmem_limit_bytes=60 * 1024 * 1024),
        name="pool",
    )(x_mid, fx_mid, gumbel, w_slice, w_temp)


def gather_sum_kernel(parts_ref, out_ref):
    mass = None
    tiles = [None] * TILES
    for chip in range(parts_ref.shape[0]):
        last = parts_ref[chip, pl.ds(FEATURES, 16), :].astype(f32)
        mass = last[: 2 * TILES] if mass is None else mass + last[: 2 * TILES]
        unit = last[2 * TILES :] * (math.log2(math.e) / SPAN)
        for t in range(TILES):
            tile = jnp.log(parts_ref[chip, pl.ds(t * DH, DH), :].astype(f32)) * unit[t : t + 1]
            tiles[t] = tile if tiles[t] is None else tiles[t] + tile
    for t in range(TILES):
        out_ref[pl.ds(t * DH, DH), :] = tiles[t]
    out_ref[pl.ds(FEATURES, 2 * TILES), :] = mass


def gather_sum(parts):
    return pl.pallas_call(
        gather_sum_kernel,
        out_shape=jax.ShapeDtypeStruct((SUMS, LANES), f32),
        in_specs=[IN_VMEM],
        out_specs=IN_VMEM,
        compiler_params=pltpu.CompilerParams(vmem_limit_bytes=16 * 1024 * 1024),
        name="gather_sum",
    )(parts)


def split(a):
    high = a.astype(bf16)
    return high, (a - high.astype(f32)).astype(bf16)


def stack_left(a):
    high, low = split(a)
    return jnp.concatenate([high, high, low, low], axis=0)


def stack_right(a):
    high, low = split(a)
    return jnp.concatenate([high, low, high, low], axis=0)


def attend_kernel(own_ref, other_ref, wq_ref, wk_ref, wv_ref, out_ref):
    core = lax.axis_index("core")
    sums = own_ref[...] + other_ref[...]
    pooled = jnp.concatenate([sums[t * DH : (t + 1) * DH] for t in range(TILES)], axis=1)
    mass = sums[FEATURES : FEATURES + TILES] + sums[FEATURES + TILES : FEATURES + 2 * TILES]
    mass = jnp.concatenate([mass[t : t + 1] for t in range(TILES)], axis=1)
    state = pooled / (mass + EPS)
    matrices = jnp.concatenate([wq_ref[...], wk_ref[...], wv_ref[...]], axis=1)
    projected = dot_tn(stack_left(matrices), stack_right(state))
    query = projected[:DH] * (1.0 / math.sqrt(DH) * LOG2E)
    key = projected[DH : 2 * DH]
    value = projected[2 * DH :]
    query = jnp.where(core == 0, query[:, :HALF], query[:, HALF:])
    scores = dot_tn(stack_left(key), stack_right(query))
    top = jnp.max(scores, axis=0, keepdims=True)
    e = jnp.exp2(scores - top)
    total = jnp.sum(e, axis=0, keepdims=True)
    both = dot(jnp.concatenate(split(value), axis=0), e.astype(bf16))
    attended = ((both[:DH] + both[DH:]) / total).astype(bf16)
    for chip in range(out_ref.shape[0]):
        out_ref[chip] = attended


def attend(chips, own, other, query_weight, key_weight, value_weight):
    return pl.pallas_call(
        attend_kernel,
        out_shape=jax.ShapeDtypeStruct((chips, DH, HALF), bf16),
        in_specs=[IN_VMEM] * 5,
        out_specs=IN_VMEM,
        compiler_params=pltpu.CompilerParams(vmem_limit_bytes=16 * 1024 * 1024),
        name="attend",
    )(own, other, query_weight, key_weight, value_weight)


def half_sums(shares_ref, attended_ref, half, pair):
    columns = pl.ds(pl.multiple_of(half * HALF, HALF), HALF)
    zero = jnp.zeros((DH, HALF), bf16)
    total = None
    for j in range(2):
        block = attended_ref[2 * pair + j]
        block = jnp.concatenate([block, zero] if j == 0 else [zero, block], axis=0)
        term = dot_nt(shares_ref[2 * pair + j, :, columns], block)
        total = term if total is None else total + term
    return total


def deslice_own_kernel(shares_ref, own_ref, out_ref):
    core = lax.axis_index("core")
    for pair in range(H // 2):
        out_ref[:, pl.ds(pair * LANES, LANES)] = half_sums(shares_ref, own_ref, core, pair)


def deslice_kernel(shares_ref, partial_ref, other_ref, out_hbm, out_ref, sems):
    core = lax.axis_index("core")
    copies = []
    for pair in range(H // 2):
        columns = pl.ds(pair * LANES, LANES)
        total = partial_ref[:, columns] + half_sums(shares_ref, other_ref, 1 - core, pair)
        out_ref[:, columns] = total.astype(bf16)
        if pair % 2:
            columns = pl.ds((pair - 1) * LANES, 2 * LANES)
            copies.append(
                pltpu.make_async_copy(out_ref.at[:, columns], out_hbm.at[:, columns], sems.at[pair // 2])
            )
            copies[-1].start()
    for copy in copies:
        copy.wait()


def deslice_own(shares, own):
    points = shares.shape[1]
    return pl.pallas_call(
        deslice_own_kernel,
        out_shape=jax.ShapeDtypeStruct((points, H * DH), f32),
        in_specs=[IN_VMEM] * 2,
        out_specs=IN_VMEM,
        compiler_params=pltpu.CompilerParams(vmem_limit_bytes=16 * 1024 * 1024),
        cost_estimate=pl.CostEstimate(
            flops=H * points * M * DH, bytes_accessed=H * points * M * 2, transcendentals=0
        ),
        name="deslice_own",
    )(shares, own)


def deslice(shares, partial, other):
    points = shares.shape[1]
    return pl.pallas_call(
        deslice_kernel,
        out_shape=jax.ShapeDtypeStruct((points, H * DH), bf16),
        in_specs=[IN_VMEM] * 3,
        out_specs=IN_HBM,
        scratch_shapes=[
            pltpu.VMEM((points, H * DH), bf16),
            pltpu.SemaphoreType.DMA((4,)),
        ],
        compiler_params=pltpu.CompilerParams(vmem_limit_bytes=16 * 1024 * 1024),
        name="deslice",
    )(shares, partial, other)


CHIPS = ("x", "y")
SWAP = [(0, 1), (1, 0)]


def on_device(x_mid, fx_mid, gumbel, w_slice, w_temp, query_weight, key_weight, value_weight):
    shares, sums = pool(x_mid, fx_mid, gumbel, w_slice, w_temp.reshape(1, DH))
    parts = lax.all_to_all(sums, CHIPS, 0, 0, tiled=True)
    own = gather_sum(parts)
    other = lax.ppermute(own, "core", SWAP)
    attended = attend(H, own, other, query_weight, key_weight, value_weight)
    attended = lax.all_to_all(attended, CHIPS, 0, 0, tiled=True)
    other = lax.ppermute(attended, "core", SWAP)
    return deslice(shares, deslice_own(shares, attended), other)


def solution(mesh):
    devices = mesh.devices
    fine = Mesh(devices.reshape(devices.shape[0], 4, 4, 2), ("dp", "x", "y", "core"))
    rows = P(("dp", "x", "y", "core"), None)
    return jax.shard_map(
        on_device,
        mesh=fine,
        in_specs=(rows, rows, rows, P(), P(), P(), P(), P()),
        out_specs=rows,
        check_vma=False,
    )
```

time: 303 us -> 57.7 us (0.19)
  blocking collectives: 125 us -> 35.9 us
  matrix products: 72.5 us -> 0 us
  other arithmetic: 53 us -> 0 us
  local copies, waits for them, and re-layouts: 19.5 us -> 0.02 us
  waiting for transfers between devices: 18.3 us -> 1.9 us
  between operations: 13.5 us -> 0.06 us
  starting transfers between devices: 0.01 us -> 9.93 us
  Pallas kernels: 0 us -> 9.67 us
    psum x1 -> x0, blocking collectives: 125 us -> none  [on_device(): pooled_features, masses = lax.psum((pooled_features, masses), 'pts')]
    dot_general x23 -> x0, matrix products: 72.5 us -> none  [the longest x8 26.4 us: attend_pair(): jnp.einsum('jqk,kjd->qjd', attn_probs, values_pair, precision=highest_pre...]
    sub x1 -> x0, other arithmetic: 47.4 us -> none  [slice_weights(): return jax.nn.softmax(logits, axis=-1)]
    all_to_all x0 -> x2, blocking collectives: none -> 35.9 us  [the longest x1 22.6 us: on_device(): parts = lax.all_to_all(sums, CHIPS, 0, 0, tiled=True)]
    psum x1 -> x0, waiting for transfers between devices: 18.3 us -> none  [on_device(): pooled_features, masses = lax.psum((pooled_features, masses), 'pts')]
    unnamed x15 -> x8, local copies, waits for them, and re-layouts: 13.8 us -> 0.02 us
    ppermute x0 -> x2, starting transfers between devices: none -> 9.93 us  [the longest x1 5.95 us: on_device(): other = lax.ppermute(own, 'core', SWAP)]
    pallas_call x0 -> x5, Pallas kernels: none -> 9.67 us  [the longest x1 6.65 us: pool(): pl.pallas_call(pool_kernel, out_shape=(jax.ShapeDtypeStruct((H, points, M...]
  transfers between devices with their start and end apart: 1 -> 2, of which waited for: 1 -> 2; matrix products, arithmetic and copies ran while one was open for 0% -> 0% of each run, Pallas kernels for 0% -> 1%
where the time goes in v1:
time: 57.7 us; the launch traced here: 57.5 us
  blocking collectives  35.9 us (62%)
  starting transfers between devices  9.93 us (17%)
  Pallas kernels  9.67 us (17%)
  waiting for transfers between devices  1.9 us (3%)
    all_to_all x1, blocking collectives, on_device(): parts = lax.all_to_all(sums, CHIPS, 0, 0, tiled=True)  22.6 us
    all_to_all x1, blocking collectives, on_device(): attended = lax.all_to_all(attended, CHIPS, 0, 0, tiled=True)  13.3 us
    pallas_call x1, Pallas kernels, pool(): pl.pallas_call(pool_kernel, out_shape=(jax.ShapeDtypeStruct((H, points, M...  6.65 us
    ppermute x1, starting transfers between devices, on_device(): other = lax.ppermute(own, 'core', SWAP)  5.95 us
    ppermute x1, starting transfers between devices, on_device(): other = lax.ppermute(attended, 'core', SWAP)  3.98 us
    pallas_call x1, Pallas kernels, deslice(): pl.pallas_call(deslice_kernel, out_shape=jax.ShapeDtypeStruct((points, H...  1.23 us
  transfers between devices with their start and end apart: 2, of which 2 were waited for; matrix products, arithmetic and copies ran while one was open for 0% of the time, Pallas kernels for 1%

profile of v1, /device:TPU:1, one launch (start us, length us, event | category | flops | bytes accessed | tf_op | source)
XLA Modules:
  0.0 57.5 jit_solution(18072516247191212864)
XLA Ops:
  0.0 0.0 copy-start.1
  0.0 0.0 copy-start.2
  0.0 0.0 copy-start.3
  0.0 6.6 %pool.1 = (bf16[16,192,512]{2,1,0:T(8,128)(2,1)}, bf16[16,272,128]{2,1,0:T(8,128)(2,1)}) custom-call(bf16[192,1024]{1,0:T(8,128)(2,1)} %x_hbm.1, bf16[192,1024]{1,0:T(8,128)(2,1)} %fx_hbm.1, bf16[192,8192]{1,0:T(8,128)(2,1)} %g_hbm.1, bf16[64,512]{1,0:T(8,128)(2,1)} %ws_hbm.1, bf16[1,64]{1,0:T(2,128)(2,1)} %bitcast.1), custom_call_target="tpu_custom_call" | custom-call | tf_op jit(solution)/shard_map/pool/pallas_call | solution.py:158
  6.7 0.0 copy-start
  6.7 22.6 %all_to_all.10.parts_ref = bf16[16,272,128]{2,1,0:T(8,128)(2,1)S(1)} all-to-all(bf16[16,272,128]{2,1,0:T(8,128)(2,1)} %get-tuple-element.8), channel_id=1, replica_groups=mesh['dp'=16,'x'=4,'y'=4,'core'=2] {'x','y'}, dimensions={0} | all-to-all | bytes 2228224 | tf_op jit(solution)/shard_map/all_to_all | solution.py:333
  29.3 0.4 gather_sum.1.own_ref
  29.7 5.9 %collective-permute-start = (f32[264,128]{1,0:T(8,128)S(1)}, f32[264,128]{1,0:T(8,128)S(1)}, u32[]{:S(2)}, u32[]{:S(2)}) collective-permute-start(f32[264,128]{1,0:T(8,128)S(1)} %gather_sum.1.own_ref), channel_id=1, source_target_pairs={{0,1},{1,0},{2,3},{3,2},{4,5},{5,4},{6,7},{7,6},{8,9},{9,8},{10,11... | collective-permute-start | bytes 405512 | tf_op jit(solution)/shard_map/ppermute | solution.py:335
  35.6 1.0 %collective-permute-done.other_ref = f32[264,128]{1,0:T(8,128)S(1)} collective-permute-done((f32[264,128]{1,0:T(8,128)S(1)}, f32[264,128]{1,0:T(8,128)S(1)}, u32[]{:S(2)}, u32[]{:S(2)}) %collective-permute-start) | collective-permute-done | bytes 135200 | tf_op jit(solution)/shard_map/ppermute | solution.py:335
  36.6 0.0 copy-done.1
  36.6 0.0 copy-done.2
  36.6 0.0 copy-done.3
  36.6 0.9 %attend.1 = bf16[16,64,256]{2,1,0:T(8,128)(2,1)S(1)} custom-call(f32[264,128]{1,0:T(8,128)S(1)} %gather_sum.1.own_ref, f32[264,128]{1,0:T(8,128)S(1)} %collective-permute-done.other_ref, f32[64,64]{1,0:T(8,128)S(1)} %copy-done.1, f32[64,64]{1,0:T(8,128)S(1)} %copy-done.2, f32[64,64]{1,0:T(8,128)S(1)} %copy-done.3), custom_call_target="tpu_custom_call" | custom-call | tf_op jit(solution)/shard_map/attend/pallas_call | solution.py:251
  37.5 13.3 %all_to_all.11.own_ref = bf16[16,64,256]{2,1,0:T(8,128)(2,1)S(1)} all-to-all(bf16[16,64,256]{2,1,0:T(8,128)(2,1)S(1)} %attend.1), channel_id=1, replica_groups=mesh['dp'=16,'x'=4,'y'=4,'core'=2] {'x','y'}, dimensions={0} | all-to-all | bytes 1048576 | tf_op jit(solution)/shard_map/all_to_all | solution.py:337
  50.8 4.0 %collective-permute-start.1 = (bf16[16,64,256]{2,1,0:T(8,128)(2,1)S(1)}, bf16[16,64,256]{2,1,0:T(8,128)(2,1)S(1)}, u32[]{:S(2)}, u32[]{:S(2)}) collective-permute-start(bf16[16,64,256]{2,1,0:T(8,128)(2,1)S(1)} %all_to_all.11.own_ref), channel_id=1, source_target_pairs={{0,1},{1,0},{2,3},{3,2},{4,5},{5,4},{6,7},{7,6},{8,9},{9,8},{10,11... | collective-permute-start | bytes 1572872 | tf_op jit(solution)/shard_map/ppermute | solution.py:338
  54.8 0.0 copy-done
  54.8 0.6 deslice_own.1.partial_ref
  55.3 0.9 %collective-permute-done.1.other_ref = bf16[16,64,256]{2,1,0:T(8,128)(2,1)S(1)} collective-permute-done((bf16[16,64,256]{2,1,0:T(8,128)(2,1)S(1)}, bf16[16,64,256]{2,1,0:T(8,128)(2,1)S(1)}, u32[]{:S(2)}, u32[]{:S(2)}) %collective-permute-start.1) | collective-permute-done | bytes 524320 | tf_op jit(solution)/shard_map/ppermute | solution.py:338
  56.3 1.2 %deslice.1 = bf16[192,1024]{1,0:T(8,128)(2,1)} custom-call(bf16[16,192,512]{2,1,0:T(8,128)(2,1)S(1)} %copy-done, f32[192,1024]{1,0:T(8,128)S(1)} %deslice_own.1.partial_ref, bf16[16,64,256]{2,1,0:T(8,128)(2,1)S(1)} %collective-permute-done.1.other_ref), custom_call_target="tpu_custom_call" | custom-call | tf_op jit(solution)/shard_map/deslice/pallas_call | solution.py:313
Async XLA Ops:
  0.0 36.6 %copy-start.1 = (f32[64,64]{1,0:T(8,128)S(1)}, f32[64,64]{1,0:T(8,128)}, u32[]{:S(2)}) copy-start(f32[64,64]{1,0:T(8,128)} %wq_ref.1) | copy-start | bytes 49156
  0.0 36.6 %copy-start.2 = (f32[64,64]{1,0:T(8,128)S(1)}, f32[64,64]{1,0:T(8,128)}, u32[]{:S(2)}) copy-start(f32[64,64]{1,0:T(8,128)} %wk_ref.1) | copy-start | bytes 49156
  0.0 36.6 %copy-start.3 = (f32[64,64]{1,0:T(8,128)S(1)}, f32[64,64]{1,0:T(8,128)}, u32[]{:S(2)}) copy-start(f32[64,64]{1,0:T(8,128)} %wv_ref.1) | copy-start | bytes 49156
  6.7 48.1 %copy-start = (bf16[16,192,512]{2,1,0:T(8,128)(2,1)S(1)}, bf16[16,192,512]{2,1,0:T(8,128)(2,1)}, u32[]{:S(2)}) copy-start(bf16[16,192,512]{2,1,0:T(8,128)(2,1)} %get-tuple-element.7.shares_ref) | copy-start | bytes 9437188
  29.7 6.9 %collective-permute-start = (f32[264,128]{1,0:T(8,128)S(1)}, f32[264,128]{1,0:T(8,128)S(1)}, u32[]{:S(2)}, u32[]{:S(2)}) collective-permute-start(f32[264,128]{1,0:T(8,128)S(1)} %gather_sum.1.own_ref), channel_id=1, source_target_pairs={{0,1},{1,0},{2,3},{3,2},{4,5},{5,4},{6,7},{7,6},{8,9},{9,8},{10,11... | collective-permute-start | bytes 405512 | tf_op jit(solution)/shard_map/ppermute | solution.py:335
  50.8 5.5 %collective-permute-start.1 = (bf16[16,64,256]{2,1,0:T(8,128)(2,1)S(1)}, bf16[16,64,256]{2,1,0:T(8,128)(2,1)S(1)}, u32[]{:S(2)}, u32[]{:S(2)}) collective-permute-start(bf16[16,64,256]{2,1,0:T(8,128)(2,1)S(1)} %all_to_all.11.own_ref), channel_id=1, source_target_pairs={{0,1},{1,0},{2,3},{3,2},{4,5},{5,4},{6,7},{7,6},{8,9},{9,8},{10,11... | collective-permute-start | bytes 1572872 | tf_op jit(solution)/shard_map/ppermute | solution.py:338

commit v2 on v1

--- a/solution.py
+++ b/solution.py
@@ -53,8 +53,8 @@
 
 
 def pool_kernel(
-    x_hbm, fx_hbm, g_hbm, ws_hbm, wt_hbm, shares_hbm, sums_hbm,
-    x_ref, fx_ref, g_ref, ws_ref, wt_ref, scale_ref, features_ref, logit_ref, shares_ref, sums_ref,
+    x_hbm, fx_hbm, g_hbm, ws_hbm, wt_ref, shares_hbm, sums_hbm,
+    x_ref, fx_ref, g_ref, ws_ref, scale_ref, features_ref, logit_ref, shares_ref, sums_ref,
     sems, g_sems, out_sems,
 ):
     points = x_hbm.shape[0]
@@ -72,21 +72,20 @@
 
     first = [
         pltpu.make_async_copy(hbm, ref, sems.at[k])
-        for k, (hbm, ref) in enumerate(((wt_hbm, wt_ref), (ws_hbm, ws_ref), (x_hbm, x_ref), (fx_hbm, fx_ref)))
+        for k, (hbm, ref) in enumerate(((ws_hbm, ws_ref), (x_hbm, x_ref), (fx_hbm, fx_ref)))
     ]
     for copy in first:
         copy.start()
     for group in range(GROUPS):
         fetch(group).start()
-    first[0].wait()
     wt = jnp.transpose(jnp.broadcast_to(wt_ref[...].astype(f32), (LANES, DH)))
     lane = lax.broadcasted_iota(jnp.int32, (DH, LANES), 1)
     wt = jnp.concatenate([jnp.where(lane == j, wt, 0.0) for j in range(H)], axis=0).astype(bf16)
-    first[1].wait()
+    first[0].wait()
     ws = ws_ref[...]
     zero = jnp.zeros_like(ws)
     ws = (jnp.concatenate([ws, zero], axis=0), jnp.concatenate([zero, ws], axis=0))
-    first[2].wait()
+    first[1].wait()
     v = dot(x_ref[...], wt)
     temper = 0.5 + jnp.maximum(v, 0.0) + jnp.log1p(jnp.exp(-jnp.abs(v)))
     scale = LOG2E / temper
@@ -97,7 +96,7 @@
         logits = dot(pairs, ws[parity])
         for p in range(H // 2):
             logit_ref[2 * p + parity] = logits[p * points : (p + 1) * points]
-    first[3].wait()
+    first[2].wait()
     features = jnp.transpose(fx_ref[...].astype(f32)).astype(bf16)
     for head in range(H):
         features_ref[head] = features[head * DH : (head + 1) * DH]
@@ -161,20 +160,19 @@
             jax.ShapeDtypeStruct((H, points, M), bf16),
             jax.ShapeDtypeStruct((H, ROWS, LANES), bf16),
         ),
-        in_specs=[IN_HBM] * 5,
+        in_specs=[IN_HBM] * 4 + [IN_VMEM],
         out_specs=(IN_HBM, IN_HBM),
         scratch_shapes=[
             pltpu.VMEM((points, H * DH), bf16),
             pltpu.VMEM((points, H * DH), bf16),
             pltpu.VMEM((GROUPS, points, GROUP * M), bf16),
             pltpu.VMEM((DH, M), bf16),
-            pltpu.VMEM((1, DH), bf16),
             pltpu.VMEM((GROUPS, points, LANES), f32),
             pltpu.VMEM((H, DH, points), bf16),
             pltpu.VMEM((H, points, M), f32),
             pltpu.VMEM((H, points, M), bf16),
             pltpu.VMEM((H, ROWS, LANES), bf16),
-            pltpu.SemaphoreType.DMA((4,)),
+            pltpu.SemaphoreType.DMA((3,)),
             pltpu.SemaphoreType.DMA((GROUPS,)),
             pltpu.SemaphoreType.DMA((2, BATCHES)),
         ],

time: 57.7 us -> 58.4 us (1.012)
  no operation moved by 1% of the time
where the time goes in v2:
time: 58.4 us; the launch traced here: 58.1 us
  blocking collectives  35.9 us (61%)
  Pallas kernels  10.2 us (17%)
  starting transfers between devices  9.93 us (17%)
  waiting for transfers between devices  1.91 us (3%)
    all_to_all x1, blocking collectives, on_device(): parts = lax.all_to_all(sums, CHIPS, 0, 0, tiled=True)  22.6 us
    all_to_all x1, blocking collectives, on_device(): attended = lax.all_to_all(attended, CHIPS, 0, 0, tiled=True)  13.3 us
    pallas_call x1, Pallas kernels, pool(): pl.pallas_call(pool_kernel, out_shape=(jax.ShapeDtypeStruct((H, points, M...  7.21 us
    ppermute x1, starting transfers between devices, on_device(): other = lax.ppermute(own, 'core', SWAP)  5.95 us
    ppermute x1, starting transfers between devices, on_device(): other = lax.ppermute(attended, 'core', SWAP)  3.98 us
    pallas_call x1, Pallas kernels, deslice(): pl.pallas_call(deslice_kernel, out_shape=jax.ShapeDtypeStruct((points, H...  1.23 us
  transfers between devices with their start and end apart: 2, of which 2 were waited for; matrix products, arithmetic and copies ran while one was open for 0% of the time, Pallas kernels for 1%

profile of v2, /device:TPU:1, one launch (start us, length us, event | category | flops | bytes accessed | tf_op | source)
XLA Modules:
  0.0 58.1 jit_solution(9280559757729732356)
XLA Ops:
  0.0 0.0 copy-start.1
  0.0 0.0 copy-start.2
  0.0 0.0 copy-start.3
  0.0 7.2 %pool.1 = (bf16[16,192,512]{2,1,0:T(8,128)(2,1)}, bf16[16,272,128]{2,1,0:T(8,128)(2,1)}) custom-call(bf16[192,1024]{1,0:T(8,128)(2,1)} %x_hbm.1, bf16[192,1024]{1,0:T(8,128)(2,1)} %fx_hbm.1, bf16[192,8192]{1,0:T(8,128)(2,1)} %g_hbm.1, bf16[64,512]{1,0:T(8,128)(2,1)} %ws_hbm.1, bf16[1,64]{1,0:T(2,128)(2,1)} %bitcast.1), custom_call_target="tpu_custom_call" | custom-call | tf_op jit(solution)/shard_map/pool/pallas_call | solution.py:157
  7.2 0.0 copy-start
  7.2 22.6 %all_to_all.10.parts_ref = bf16[16,272,128]{2,1,0:T(8,128)(2,1)S(1)} all-to-all(bf16[16,272,128]{2,1,0:T(8,128)(2,1)} %get-tuple-element.8), channel_id=1, replica_groups=mesh['dp'=16,'x'=4,'y'=4,'core'=2] {'x','y'}, dimensions={0} | all-to-all | bytes 2228224 | tf_op jit(solution)/shard_map/all_to_all | solution.py:331
  29.8 0.4 gather_sum.1.own_ref
  30.2 6.0 %collective-permute-start = (f32[264,128]{1,0:T(8,128)S(1)}, f32[264,128]{1,0:T(8,128)S(1)}, u32[]{:S(2)}, u32[]{:S(2)}) collective-permute-start(f32[264,128]{1,0:T(8,128)S(1)} %gather_sum.1.own_ref), channel_id=1, source_target_pairs={{0,1},{1,0},{2,3},{3,2},{4,5},{5,4},{6,7},{7,6},{8,9},{9,8},{10,11... | collective-permute-start | bytes 405512 | tf_op jit(solution)/shard_map/ppermute | solution.py:333
  36.2 1.0 %collective-permute-done.other_ref = f32[264,128]{1,0:T(8,128)S(1)} collective-permute-done((f32[264,128]{1,0:T(8,128)S(1)}, f32[264,128]{1,0:T(8,128)S(1)}, u32[]{:S(2)}, u32[]{:S(2)}) %collective-permute-start) | collective-permute-done | bytes 135200 | tf_op jit(solution)/shard_map/ppermute | solution.py:333
  37.1 0.0 copy-done.1
  37.1 0.0 copy-done.2
  37.1 0.0 copy-done.3
  37.1 0.9 %attend.1 = bf16[16,64,256]{2,1,0:T(8,128)(2,1)S(1)} custom-call(f32[264,128]{1,0:T(8,128)S(1)} %gather_sum.1.own_ref, f32[264,128]{1,0:T(8,128)S(1)} %collective-permute-done.other_ref, f32[64,64]{1,0:T(8,128)S(1)} %copy-done.1, f32[64,64]{1,0:T(8,128)S(1)} %copy-done.2, f32[64,64]{1,0:T(8,128)S(1)} %copy-done.3), custom_call_target="tpu_custom_call" | custom-call | tf_op jit(solution)/shard_map/attend/pallas_call | solution.py:249
  38.0 13.3 %all_to_all.11.own_ref = bf16[16,64,256]{2,1,0:T(8,128)(2,1)S(1)} all-to-all(bf16[16,64,256]{2,1,0:T(8,128)(2,1)S(1)} %attend.1), channel_id=1, replica_groups=mesh['dp'=16,'x'=4,'y'=4,'core'=2] {'x','y'}, dimensions={0} | all-to-all | bytes 1048576 | tf_op jit(solution)/shard_map/all_to_all | solution.py:335
  51.3 4.0 %collective-permute-start.1 = (bf16[16,64,256]{2,1,0:T(8,128)(2,1)S(1)}, bf16[16,64,256]{2,1,0:T(8,128)(2,1)S(1)}, u32[]{:S(2)}, u32[]{:S(2)}) collective-permute-start(bf16[16,64,256]{2,1,0:T(8,128)(2,1)S(1)} %all_to_all.11.own_ref), channel_id=1, source_target_pairs={{0,1},{1,0},{2,3},{3,2},{4,5},{5,4},{6,7},{7,6},{8,9},{9,8},{10,11... | collective-permute-start | bytes 1572872 | tf_op jit(solution)/shard_map/ppermute | solution.py:336
  55.3 0.0 copy-done
  55.3 0.6 deslice_own.1.partial_ref
  55.9 0.9 %collective-permute-done.1.other_ref = bf16[16,64,256]{2,1,0:T(8,128)(2,1)S(1)} collective-permute-done((bf16[16,64,256]{2,1,0:T(8,128)(2,1)S(1)}, bf16[16,64,256]{2,1,0:T(8,128)(2,1)S(1)}, u32[]{:S(2)}, u32[]{:S(2)}) %collective-permute-start.1) | collective-permute-done | bytes 524320 | tf_op jit(solution)/shard_map/ppermute | solution.py:336
  56.8 1.2 %deslice.1 = bf16[192,1024]{1,0:T(8,128)(2,1)} custom-call(bf16[16,192,512]{2,1,0:T(8,128)(2,1)S(1)} %copy-done, f32[192,1024]{1,0:T(8,128)S(1)} %deslice_own.1.partial_ref, bf16[16,64,256]{2,1,0:T(8,128)(2,1)S(1)} %collective-permute-done.1.other_ref), custom_call_target="tpu_custom_call" | custom-call | tf_op jit(solution)/shard_map/deslice/pallas_call | solution.py:311
Async XLA Ops:
  0.0 37.1 %copy-start.1 = (f32[64,64]{1,0:T(8,128)S(1)}, f32[64,64]{1,0:T(8,128)}, u32[]{:S(2)}) copy-start(f32[64,64]{1,0:T(8,128)} %wq_ref.1) | copy-start | bytes 49156
  0.0 37.1 %copy-start.2 = (f32[64,64]{1,0:T(8,128)S(1)}, f32[64,64]{1,0:T(8,128)}, u32[]{:S(2)}) copy-start(f32[64,64]{1,0:T(8,128)} %wk_ref.1) | copy-start | bytes 49156
  0.0 37.1 %copy-start.3 = (f32[64,64]{1,0:T(8,128)S(1)}, f32[64,64]{1,0:T(8,128)}, u32[]{:S(2)}) copy-start(f32[64,64]{1,0:T(8,128)} %wv_ref.1) | copy-start | bytes 49156
  7.2 48.1 %copy-start = (bf16[16,192,512]{2,1,0:T(8,128)(2,1)S(1)}, bf16[16,192,512]{2,1,0:T(8,128)(2,1)}, u32[]{:S(2)}) copy-start(bf16[16,192,512]{2,1,0:T(8,128)(2,1)} %get-tuple-element.7.shares_ref) | copy-start | bytes 9437188
  30.2 6.9 %collective-permute-start = (f32[264,128]{1,0:T(8,128)S(1)}, f32[264,128]{1,0:T(8,128)S(1)}, u32[]{:S(2)}, u32[]{:S(2)}) collective-permute-start(f32[264,128]{1,0:T(8,128)S(1)} %gather_sum.1.own_ref), channel_id=1, source_target_pairs={{0,1},{1,0},{2,3},{3,2},{4,5},{5,4},{6,7},{7,6},{8,9},{9,8},{10,11... | collective-permute-start | bytes 405512 | tf_op jit(solution)/shard_map/ppermute | solution.py:333
  51.3 5.5 %collective-permute-start.1 = (bf16[16,64,256]{2,1,0:T(8,128)(2,1)S(1)}, bf16[16,64,256]{2,1,0:T(8,128)(2,1)S(1)}, u32[]{:S(2)}, u32[]{:S(2)}) collective-permute-start(bf16[16,64,256]{2,1,0:T(8,128)(2,1)S(1)} %all_to_all.11.own_ref), channel_id=1, source_target_pairs={{0,1},{1,0},{2,3},{3,2},{4,5},{5,4},{6,7},{7,6},{8,9},{9,8},{10,11... | collective-permute-start | bytes 1572872 | tf_op jit(solution)/shard_map/ppermute | solution.py:336
